TPU v7x, 256 devices: a whole 4x4x8 slice. The times are simulated.
256 devices in a mesh: group: 16 (over z, core), member: 16 (over x, y).
Axes of the slice: x: 4, y: 4, z: 8, core: 2. Of those that a mesh axis runs over, the one named last changes fastest.
Arguments:
- features: float32 [98304, 256], P(('group', 'member')), may hold values from 0.01 to 9
- tiles: float32 [24576, 128, 128], P(('group', 'member')), may hold values from 0 to 1.5, as said below
- tile_col: int32 [24576], P(('group', 'member')), may hold values from 0 to 47
- tile_slot: int32 [24576], P(('group', 'member')), may hold values from 0 to 31
- mirror_list: int32 [256, 16, 2], P(('group', 'member')), may hold values from 0 to 2, as said below
- tile_counts: int32 [256], P(('group', 'member')), may hold values from 64 to 96, as said below
- self_weight: float32 [2, 256, 256], replicated, may hold values from -0.375 to 0.375
- neigh_weight: float32 [2, 256, 256], replicated, may hold values from -0.375 to 0.375
Outputs:
- embeddings: float32 [98304, 256], P(('group', 'member'))
Inputs may be any that keep to these rules, and one draw needn't show every extreme that they name: `tiles`: positive edge weights. `tile_col`: an index among the 48 blocks of the tile's group. `tile_slot`: an index among the device's 32 mirror slots. `mirror_list`: the 2 entries of one device and one destination group differ. `tile_counts`: some device has all 96 tiles live.
All inputs are finite; a program needn't handle non-finite values.
Results may differ from a plain program's by a relative error of at most 0.0003.
Values sent between devices are 32-bit elements; how exact they have to be, the bound alone decides.
No kernel may reach another device: no remote copies, remote signals or barrier semaphores. Data moves between devices by JAX's collectives and lax.ppermute only.
A program may use at most 128 MiB of HBM per device.

v0:
```python
import jax
import jax.numpy as jnp
from jax import lax
from jax.sharding import PartitionSpec as P

F = 256
TILE = 128
LAYERS = 2
BLK_DEV = 3
TILES_DEV = 96
CAP = 2


def body(features, tiles, tile_col, tile_slot, mirror_list, tile_counts, self_weight, neigh_weight):
    groups = lax.axis_size("group")
    members = lax.axis_size("member")
    mirror = mirror_list[0]
    positions = jnp.arange(TILES_DEV, dtype=jnp.int32)
    live = (positions < tile_counts[0]).astype(jnp.float32)
    dest_group = tile_slot // CAP
    target = dest_group * BLK_DEV + mirror[dest_group, tile_slot % CAP]
    labels = jnp.arange(groups * BLK_DEV, dtype=jnp.int32)
    onehot = (target[None, :] == labels[:, None]).astype(jnp.float32) * live[None, :]
    degree_part = jnp.dot(onehot, jnp.sum(tiles, axis=2), precision=lax.Precision.HIGHEST)
    state = features
    for layer in range(LAYERS):
        gathered = lax.all_gather(state, "member", axis=0, tiled=True).reshape(
            members * BLK_DEV, TILE, F
        )
        sources = jnp.take(gathered, tile_col, axis=0)
        prods = jnp.einsum("tij,tjf->tif", tiles, sources, precision=lax.Precision.HIGHEST)
        partial_value = jnp.einsum("nt,tif->nif", onehot, prods, precision=lax.Precision.HIGHEST)
        summed, degree = (
            lax.psum_scatter(partial_value, "group", scatter_dimension=0, tiled=True),
            lax.psum_scatter(degree_part, "group", scatter_dimension=0, tiled=True),
        )
        summed = summed.reshape(BLK_DEV * TILE, F)
        degree = degree.reshape(BLK_DEV * TILE)
        neighbour_mean = (state + summed) / (1.0 + degree)[:, None]
        activated = jax.nn.relu(
            jnp.dot(state, self_weight[layer], precision=lax.Precision.HIGHEST)
            + jnp.dot(neighbour_mean, neigh_weight[layer], precision=lax.Precision.HIGHEST)
        )
        state = activated * lax.rsqrt(
            jnp.mean(activated * activated, axis=1, keepdims=True) + 1e-05
        )
    return state


def solution(mesh):
    placed = (
        P(("group", "member"), None),
        P(("group", "member"), None, None),
        P(("group", "member")),
        P(("group", "member")),
        P(("group", "member"), None, None),
        P(("group", "member")),
        P(),
        P(),
    )
    return jax.shard_map(
        body, mesh=mesh, in_specs=placed, out_specs=P(("group", "member"), None), check_vma=False
    )
```

profile of v0, /device:TPU:24, one launch (start us, length us, event | category | flops | bytes accessed | tf_op | source)
XLA Modules:
  0.0 431.3 jit_solution(8466189959982422728)
XLA Ops:
  6.5 0.7 all-gather.3.cloned.1.call-update
  8.6 1.5 gather_fusion
  11.5 67.4 %all-gather.3.cloned.1.call-done = f32[6144,256]{1,0:T(8,128)} async-done(((f32[384,256]{1,0:T(8,128)}), f32[6144,256]{1,0:T(8,128)}) %all-gather.3.cloned.1.call-update) | async-done | bytes 6291472 | tf_op jit(solution)/shard_map/all_gather | solution.py:27
  78.9 11.5 %gather_fusion.1 = f32[96,128,256]{2,1,0:T(8,128)} fusion(f32[48,128,256]{2,1,0:T(8,128)} %bitcast.43, s32[1024]{0:T(1024)S(1)} %pad_clamp_fusion), kind=kCustom, calls=%fused_computation.clone | custom fusion | bytes 25166208 | tf_op jit(solution)/shard_map/jit(_take)/gather | solution.py:30
  90.3 27.1 %fusion.8 = f32[96,128,256]{1,2,0:T(8,128)} fusion(f32[96,128,128]{2,1,0:T(8,128)} %param.11, f32[96,128,256]{2,1,0:T(8,128)} %gather_fusion.1, pred[96]{0:T(512)(128)(4,1)S(1)} %compare_and_fusion), kind=kOutput, calls=%fused_computation.11 | convolution fusion | flops 4834983936 | bytes 31457376 | tf_op jit(solution)/shard_map/tij,tjf->tif/dot_general | solution.py:31
  117.5 12.7 %copy.31 = f32[96,128,256]{2,0,1:T(8,128)} copy(f32[96,128,256]{1,2,0:T(8,128)} %fusion.8) | data formatting | bytes 25165824 | tf_op jit(solution)/shard_map/tij,tjf->tif/dot_general | solution.py:31
  130.1 9.8 %fusion.35 = f32[48,128,256]{2,0,1:T(8,128)S(1)} fusion(f32[96,128,256]{2,0,1:T(8,128)} %copy.31, f32[96]{0:T(128)S(1)} %compare_convert_fusion, s32[96]{0:T(128)S(1)} %multiply_add_fusion), kind=kOutput, calls=%fused_computation.41 | convolution fusion | flops 1811948544 | bytes 18875136 | tf_op jit(solution)/shard_map/nt,tif->nif/dot_general | solution.py:32
  140.0 6.3 %copy.32 = f32[48,128,256]{2,1,0:T(8,128)} copy(f32[48,128,256]{2,0,1:T(8,128)S(1)} %fusion.35) | data formatting | bytes 12582912 | tf_op jit(solution)/shard_map/nt,tif->nif/dot_general | solution.py:32
  146.5 4.5 %reduce_sum.27 = f32[96,128]{1,0:T(8,128)S(1)} reduce(f32[96,128,128]{2,1,0:T(8,128)} %param.11, f32[]{:T(128)} %constant.52.clone.1), dimensions={2}, to_apply=%region_1.3 | reduce | flops 1560576 | bytes 6340612 | tf_op jit(solution)/shard_map/reduce_sum | solution.py:24
  152.5 48.7 %all-reduce = f32[48,128]{1,0:T(8,128)S(1)} all-reduce(f32[48,128]{1,0:T(8,128)S(1)} %fusion.32), channel_id=3, replica_groups=mesh['group'=16,'member'=16] {'group'}, use_global_device_ids=true, to_apply=%region_2.4.clone | all-reduce | flops 6144 | bytes 49152
  201.8 11.4 %reduce-scatter.3.cloned.1.call-done = f32[3,128,256]{2,1,0:T(8,128)} async-done(((f32[48,128,256]{2,1,0:T(8,128)}), f32[3,128,256]{2,1,0:T(8,128)}) %reduce-scatter.3.cloned.1.call-update) | async-done | bytes 393232 | tf_op jit(solution)/shard_map/reduce_scatter | solution.py:34
  213.2 1.2 copy.34
  215.0 0.8 broadcast_multiply_fusion.1
  215.9 64.8 %all-gather.5.cloned.1.call-done = f32[6144,256]{0,1:T(8,128)} async-done(((f32[384,256]{0,1:T(8,128)}), f32[6144,256]{0,1:T(8,128)}) %all-gather.5.cloned.1.call-update) | async-done | bytes 6291472 | tf_op jit(solution)/shard_map/all_gather | solution.py:27
  280.7 6.7 %copy.43 = f32[6144,256]{1,0:T(8,128)} copy(f32[6144,256]{0,1:T(8,128)} %all-gather.5.cloned.1.call-done) | data formatting | bytes 12582912 | tf_op jit(solution)/shard_map/reshape | solution.py:27
  287.4 11.5 %gather_fusion.2 = f32[96,128,256]{2,1,0:T(8,128)} fusion(f32[48,128,256]{2,1,0:T(8,128)} %bitcast.42, s32[1024]{0:T(1024)S(1)} %pad_clamp_fusion), kind=kCustom, calls=%fused_computation.1.clone | custom fusion | bytes 25166208 | tf_op jit(solution)/shard_map/jit(_take)/gather | solution.py:30
  298.9 27.1 %fusion.11 = f32[96,128,256]{1,2,0:T(8,128)} fusion(f32[96,128,128]{2,1,0:T(8,128)} %param.11, f32[96,128,256]{2,1,0:T(8,128)} %gather_fusion.2, pred[96]{0:T(512)(128)(4,1)S(1)} %compare_and_fusion), kind=kOutput, calls=%fused_computation.12 | convolution fusion | flops 4834983936 | bytes 31457376 | tf_op jit(solution)/shard_map/tij,tjf->tif/dot_general | solution.py:31
  326.0 12.7 %copy.37 = f32[96,128,256]{2,0,1:T(8,128)} copy(f32[96,128,256]{1,2,0:T(8,128)} %fusion.11) | data formatting | bytes 25165824 | tf_op jit(solution)/shard_map/tij,tjf->tif/dot_general | solution.py:31
  338.7 9.9 %fusion.34 = f32[48,128,256]{2,0,1:T(8,128)S(1)} fusion(f32[96,128,256]{2,0,1:T(8,128)} %copy.37, f32[96]{0:T(128)S(1)} %compare_convert_fusion, s32[96]{0:T(128)S(1)} %multiply_add_fusion), kind=kOutput, calls=%fused_computation.40 | convolution fusion | flops 1811948544 | bytes 18875136 | tf_op jit(solution)/shard_map/nt,tif->nif/dot_general | solution.py:32
  348.5 6.3 %copy.38 = f32[48,128,256]{2,1,0:T(8,128)} copy(f32[48,128,256]{2,0,1:T(8,128)S(1)} %fusion.34) | data formatting | bytes 12582912 | tf_op jit(solution)/shard_map/nt,tif->nif/dot_general | solution.py:32
  355.5 66.0 %reduce-scatter.5.cloned.1.call-done = f32[3,128,256]{2,1,0:T(8,128)} async-done(((f32[48,128,256]{2,1,0:T(8,128)}), f32[3,128,256]{2,1,0:T(8,128)}) %reduce-scatter.5.cloned.1.call-update) | async-done | bytes 393232 | tf_op jit(solution)/shard_map/reduce_scatter | solution.py:34
  421.5 1.2 copy.39
  422.7 0.7 multiply_reduce_fusion
  423.4 0.9 copy.40
  (37 shorter events, 5.2 us)
Async XLA Ops:
  6.5 2.1 copy-start
  6.5 72.3 %all-gather.3.cloned.1.call-start = ((), (), s32[]{:S(2)}) async-start(), calls=%async_computation.2 | async-start | bytes 6684672 | tf_op jit(solution)/shard_map/all_gather | solution.py:27
  7.3 205.9 %reduce-scatter.3.cloned.1.call-start = ((), (), s32[]{:S(2)}) async-start(), calls=%async_computation.3 | async-start | bytes 6684672 | tf_op jit(solution)/shard_map/reduce_scatter | solution.py:34
  139.9 6.4 %copy-start.2 = (f32[384,256]{1,0:T(8,128)S(1)}, f32[384,256]{1,0:T(8,128)}, u32[]{:S(2)}) copy-start(f32[384,256]{1,0:T(8,128)} %param.10) | copy-start | bytes 1179652
  139.9 11.1 %copy-start.6 = (u32[256]{0:T(256)S(1)}, u32[256]{0:T(256)}, u32[]{:S(2)}) copy-start(u32[256]{0:T(256)} %constant.77) | copy-start | bytes 3076
  140.0 61.2 %copy-start.4 = (f32[2,256,256]{2,1,0:T(8,128)S(1)}, f32[2,256,256]{2,1,0:T(8,128)}, u32[]{:S(2)}) copy-start(f32[2,256,256]{2,1,0:T(8,128)} %param.16) | copy-start | bytes 1572868
  140.0 74.4 %copy-start.5 = (f32[2,256,256]{2,1,0:T(8,128)S(1)}, f32[2,256,256]{2,1,0:T(8,128)}, u32[]{:S(2)}) copy-start(f32[2,256,256]{2,1,0:T(8,128)} %param.17) | copy-start | bytes 1572868
  146.3 134.3 %all-gather.5.cloned.1.call-start = ((), (), s32[]{:S(2)}) async-start(), calls=%async_computation.4 | async-start | bytes 6684672 | tf_op jit(solution)/shard_map/all_gather | solution.py:27
  215.8 205.7 %reduce-scatter.5.cloned.1.call-start = ((), (), s32[]{:S(2)}) async-start(), calls=%async_computation.5 | async-start | bytes 6684672 | tf_op jit(solution)/shard_map/reduce_scatter | solution.py:34
  338.7 85.7 %copy-start.1 = (s32[1,16,2]{1,2,0:T(2,128)S(1)}, s32[1,16,2]{1,2,0:T(2,128)}, u32[]{:S(2)}) copy-start(s32[1,16,2]{1,2,0:T(2,128)} %param.14) | copy-start | bytes 388
  348.5 6.3 %copy-start.3 = (f32[384,256]{0,1:T(8,128)S(1)}, f32[384,256]{0,1:T(8,128)}, u32[]{:S(2)}) copy-start(f32[384,256]{0,1:T(8,128)} %broadcast_multiply_fusion.1) | copy-start | bytes 1179652
Sparse Core Ops, SparseCore 0:
  9.8 68.9 all-gather.2
  146.4 66.6 reduce-scatter.2
  216.0 64.6 all-gather.4
  355.0 66.4 reduce-scatter.4
where the time goes:
time: 440 us; the launch traced here: 431 us
  waiting for transfers between devices  210 us (48%)
  matrix products  76.7 us (17%)
  local copies, waits for them, and re-layouts  73.2 us (17%)
  blocking collectives  48.7 us (11%)
  between operations  15.1 us (3%)
  other arithmetic  7.33 us (2%)
    all_gather x2, waiting for transfers between devices, body(): lax.all_gather(state, 'member', axis=0, tiled=True)  132 us
    reduce_scatter x2, waiting for transfers between devices, body(): lax.psum_scatter(partial_value, 'group', scatter_dimension=0, tiled=True)  77.4 us
    dot_general x2, matrix products, body(): jnp.einsum('tij,tjf->tif', tiles, sources, precision=lax.Precision.HIGHEST)  54.2 us
    unnamed x1, blocking collectives  48.7 us
    dot_general x2, local copies, waits for them, and re-layouts, body(): jnp.einsum('tij,tjf->tif', tiles, sources, precision=lax.Precision.HIGHEST)  25.4 us
    gather x2, local copies, waits for them, and re-layouts, body(): sources = jnp.take(gathered, tile_col, axis=0)  22.9 us
    dot_general x2, matrix products, body(): jnp.einsum('nt,tif->nif', onehot, prods, precision=lax.Precision.HIGHEST)  19.6 us
    dot_general x2, local copies, waits for them, and re-layouts, body(): jnp.einsum('nt,tif->nif', onehot, prods, precision=lax.Precision.HIGHEST)  12.6 us
  transfers between devices with their start and end apart: 4, of which 4 were waited for; matrix products, arithmetic and copies ran while one was open for 2% of the time, Pallas kernels for 0%

commit v1 on v0

v1 whole, which is shorter than its diff:
```python
import functools

import jax
import jax.numpy as jnp
from jax import lax
from jax.experimental import pallas as pl
from jax.experimental.pallas import tpu as pltpu
from jax.sharding import Mesh
from jax.sharding import PartitionSpec as P

F = 256
TILE = 128
LAYERS = 2
BLK_DEV = 3
TILES_DEV = 96
CAP = 2
NZ, NC, NX, NY = 8, 2, 4, 4
AXES = ("z", "c", "x", "y")
UNROLL = 4
SLOTS = TILES_DEV + 4 * UNROLL
ROWS = BLK_DEV * TILE
BF = jnp.bfloat16
F32 = jnp.float32
VMEM = pl.BlockSpec(memory_space=pltpu.VMEM)
SMEM = pl.BlockSpec(memory_space=pltpu.SMEM)


def perm(step):
    pairs = []
    for z in range(NZ):
        for c in range(NC):
            for x in range(NX):
                for y in range(NY):
                    tz, tc, tx, ty = step(z, c, x, y)
                    pairs.append((
                        ((z * NC + c) * NX + x) * NY + y,
                        (((tz % NZ) * NC + tc % NC) * NX + tx % NX) * NY + ty % NY,
                    ))
    return pairs


PAIR = perm(lambda z, c, x, y: (z, c + 1, x, y))


def along_z(d):
    return perm(lambda z, c, x, y: (z + (d if c == 0 else -d), c, x, y))


def in_plane(d, phase):
    return perm(lambda z, c, x, y: (z, c, x + d, y) if (c + phase) % 2 == 0 else (z, c, x, y + d))


def send(value, pairs):
    return lax.ppermute(value, AXES, pairs)


def split(value):
    high = value.astype(BF)
    return high, (value - high.astype(F32)).astype(BF)


def slot_of(offset):
    return jnp.where(offset == 0, 0, jnp.where(offset == 3, 1, jnp.where(offset == 1, 2, 3)))


def late_piece(r):
    return jnp.where(
        r == 3, 0, jnp.where(r == 6, 1, jnp.where(r == 2, 2, jnp.where(r == 7, 3, jnp.where(r == 1, 4, 5))))
    )


def prepare_kernel(place, col, slot, mirror, count, tiles, source, dest, bounds, order, split_tiles, degree, cls, dst, nxt):
    z, c, p, q = place[0], place[1], place[2], place[3]
    for s in range(4):
        nxt[s] = 0

    def classify(t, _):
        sl = slot[t]
        g = sl // CAP
        k = mirror[sl]
        gz, gc = g // NC, g % NC
        r = lax.rem(jnp.where(gc == 0, gz - z, z - gz) + NZ, NZ)
        kept = (gc == c).astype(jnp.int32)
        early = jnp.logical_or(r == 4, r == 5)
        seg = jnp.where(early, 0, 2) + kept
        piece = jnp.where(early, r - 4, late_piece(r))
        live = t < count[0]
        seg = jnp.where(live, seg, 4)
        cls[t] = seg
        dst[t] = piece * 4 + k

        @pl.when(live)
        def _():
            nxt[seg] = nxt[seg] + 1

        return 0

    lax.fori_loop(0, TILES_DEV, classify, 0)
    start = jnp.int32(0)
    for s in range(4):
        chunks = (nxt[s] + UNROLL - 1) // UNROLL
        bounds[s] = start // UNROLL
        nxt[s] = start
        start = start + chunks * UNROLL
    bounds[4] = start // UNROLL

    def clear(s, _):
        order[s] = TILES_DEV
        source[s] = 0
        dest[s] = 0
        return 0

    lax.fori_loop(0, SLOTS, clear, 0)

    def place_tile(t, _):
        seg = cls[t]

        @pl.when(seg < 4)
        def _():
            at = nxt[seg]
            nxt[seg] = at + 1
            b = col[t]
            m, j = b // BLK_DEV, b % BLK_DEV
            bx, by = m // NY, m % NY
            bp = jnp.where(c == 0, bx, by)
            bq = jnp.where(c == 0, by, bx)
            sp = slot_of(lax.rem(bp - p + 4, 4))
            sq = slot_of(lax.rem(bq - q + 4, 4))
            order[at] = t
            source[at] = sq * 12 + sp * 3 + j
            dest[at] = dst[t]

        return 0

    lax.fori_loop(0, TILES_DEV, place_tile, 0)
    degree[...] = jnp.zeros_like(degree)
    ones = jnp.ones((8, TILE), BF)

    def chunk(i, _):
        for u in range(UNROLL):
            s = i * UNROLL + u
            t = order[s]
            live = (t < TILES_DEV).astype(F32)
            high, low = split(tiles[jnp.minimum(t, TILES_DEV - 1)] * live)
            split_tiles[s, :, 0:TILE] = high
            split_tiles[s, :, TILE : 2 * TILE] = low
            nt = (((1,), (1,)), ((), ()))
            row = lax.dot_general(ones, high, nt, preferred_element_type=F32) + lax.dot_general(
                ones, low, nt, preferred_element_type=F32
            )
            seg = (
                (i >= bounds[1]).astype(jnp.int32)
                + (i >= bounds[2]).astype(jnp.int32)
                + (i >= bounds[3]).astype(jnp.int32)
            )
            d = dest[s]
            piece, k = d // 4, d % 4
            at = piece + jnp.where(seg == 0, 0, jnp.where(seg == 1, 2, jnp.where(seg == 2, 4, 10)))
            degree[at, pl.ds(k, 1), :] += row[0:1]
        return 0

    lax.fori_loop(0, bounds[4], chunk, 0)


def prepare(place, col, slot, mirror, count, tiles):
    return pl.pallas_call(
        prepare_kernel,
        out_shape=(
            jax.ShapeDtypeStruct((SLOTS,), jnp.int32),
            jax.ShapeDtypeStruct((SLOTS,), jnp.int32),
            jax.ShapeDtypeStruct((8,), jnp.int32),
            jax.ShapeDtypeStruct((SLOTS,), jnp.int32),
            jax.ShapeDtypeStruct((SLOTS, TILE, 2 * TILE), BF),
            jax.ShapeDtypeStruct((16, 8, TILE), F32),
        ),
        in_specs=[SMEM] * 5 + [VMEM],
        out_specs=(SMEM, SMEM, SMEM, SMEM, VMEM, VMEM),
        scratch_shapes=[
            pltpu.SMEM((TILES_DEV,), jnp.int32),
            pltpu.SMEM((TILES_DEV,), jnp.int32),
            pltpu.SMEM((8,), jnp.int32),
        ],
        compiler_params=pltpu.CompilerParams(vmem_limit_bytes=20 << 20),
        cost_estimate=pl.CostEstimate(flops=10**8, bytes_accessed=13 * 10**6, transcendentals=0),
        name="prepare",
    )(place, col, slot, mirror, count, tiles)


def product_kernel(first, n, rows, source, dest, bounds, degree, tiles, *refs):
    gathered, (sent, kept), (high, low) = refs[:5], refs[5:7], refs[7:]
    base = 0
    for ref in gathered:
        blocks = ref.shape[0] // TILE

        def load(i, _, ref=ref, base=base):
            high[base + i], low[base + i] = split(ref[pl.ds(pl.multiple_of(i * TILE, TILE), TILE), :])
            return 0

        lax.fori_loop(0, blocks, load, 0)
        base += blocks
    for part, out in enumerate((sent, kept)):
        out[...] = jnp.zeros_like(out)
        if rows > ROWS:
            for i in range(n):
                out[i, ROWS:rows, 0:TILE] = degree[(0 if n == 2 else 4) + part * n + i]

        def chunk(i, _, out=out):
            for u in range(UNROLL):
                s = i * UNROLL + u
                b = source[s]
                both = tiles[s]
                value = jnp.dot(
                    jnp.concatenate([both, both[:, :TILE]], axis=1),
                    jnp.concatenate([high[b], high[b], low[b]], axis=0),
                    preferred_element_type=F32,
                )
                d = dest[s]
                piece, k = d // 4, d % 4
                at = pl.ds(pl.multiple_of(k * TILE, TILE), TILE)
                out[piece, at, :] += value
            return 0

        lax.fori_loop(bounds[first + part], bounds[first + part + 1], chunk, 0)


def products(first, n, rows, plan, gathered):
    source, dest, bounds, degree, tiles = plan
    return pl.pallas_call(
        functools.partial(product_kernel, first, n, rows),
        out_shape=(jax.ShapeDtypeStruct((n, rows, F), F32),) * 2,
        in_specs=[SMEM] * 3 + [VMEM] * 7,
        out_specs=(VMEM, VMEM),
        scratch_shapes=[pltpu.VMEM((48, TILE, F), BF)] * 2,
        compiler_params=pltpu.CompilerParams(vmem_limit_bytes=32 << 20),
        cost_estimate=pl.CostEstimate(flops=4 * 10**9 * n // 8, bytes_accessed=15 * 10**6, transcendentals=0),
        name="early" if n == 2 else "late",
    )(source, dest, bounds, degree, tiles, *gathered)


def gather(state):
    a, b, c = (send(state, in_plane(d, 0)) for d in (1, -1, 2))
    own = jnp.concatenate([state, a, b, c], axis=0)
    a, b = send(own, in_plane(1, 1)), send(own, in_plane(-1, 1))
    half = own.shape[0] // 2
    return own, a, b, send(a[:half], in_plane(1, 1)), send(b[half:], in_plane(-1, 1))


def body(features, tiles, tile_col, tile_slot, mirror_list, tile_counts, self_weight, neigh_weight):
    z, c, x, y = (lax.axis_index(a).astype(jnp.int32) for a in AXES)
    place = jnp.stack([z, c, jnp.where(c == 0, x, y), jnp.where(c == 0, y, x)])
    source, dest, bounds, _, split_tiles, degree_part = prepare(
        place, tile_col, tile_slot, mirror_list.reshape(-1), tile_counts, tiles
    )
    plan = (source, dest, bounds, degree_part, split_tiles)
    up, down = along_z(1), along_z(-1)
    state = features
    for layer in range(LAYERS):
        rows = ROWS + 8 if layer == 0 else ROWS
        gathered = gather(state)
        sent, kept = products(0, 2, rows, plan, gathered)
        got = send(sent, PAIR)
        f = send(kept[0] + got[0], up)
        g = send(kept[1] + got[1], down)
        sent, kept = products(2, 6, rows, plan, gathered)
        got = send(sent, PAIR)
        f = send(f + (kept[0] + got[0]), up)
        g = send(g + (kept[1] + got[1]), down)
        f = send(f + (kept[2] + got[2]), up)
        g = send(g + (kept[3] + got[3]), down)
        f = send(f + (kept[4] + got[4]), up)
        total = f + (g + (kept[5] + got[5]))
        if layer == 0:
            degree = total[ROWS : ROWS + BLK_DEV, :TILE].reshape(ROWS)
            total = total[:ROWS]
        neighbour_mean = (state + total) / (1.0 + degree)[:, None]
        activated = jax.nn.relu(
            jnp.dot(state, self_weight[layer], precision=lax.Precision.HIGHEST)
            + jnp.dot(neighbour_mean, neigh_weight[layer], precision=lax.Precision.HIGHEST)
        )
        state = activated * lax.rsqrt(jnp.mean(activated * activated, axis=1, keepdims=True) + 1e-05)
    return state


def solution(mesh):
    fine = Mesh(mesh.devices.reshape(NZ, NC, NX, NY), AXES)
    placed = (
        P(AXES, None),
        P(AXES, None, None),
        P(AXES),
        P(AXES),
        P(AXES, None, None),
        P(AXES),
        P(),
        P(),
    )
    return jax.shard_map(body, mesh=fine, in_specs=placed, out_specs=P(AXES, None), check_vma=False)
```

time: 440 us -> 235 us (0.53); the launches traced: 431 us -> 231 us
  matrix products: 76.7 us -> 2.21 us
  waiting for transfers between devices: 210 us -> 141 us
  local copies, waits for them, and re-layouts: 73.2 us -> 6.13 us
  blocking collectives: 48.7 us -> 0 us
  starting transfers between devices: 0.12 us -> 43.9 us
  Pallas kernels: 0 us -> 34.5 us
  between operations: 15.1 us -> 0.95 us
  other arithmetic: 7.33 us -> 2.35 us
    ppermute x0 -> x32, waiting for transfers between devices: none -> 141 us  [send(): return lax.ppermute(value, AXES, pairs)]
    all_gather x2 -> x0, waiting for transfers between devices: 132 us -> none  [body(): lax.all_gather(state, 'member', axis=0, tiled=True)]
    reduce_scatter x2 -> x0, waiting for transfers between devices: 77.4 us -> none  [body(): lax.psum_scatter(partial_value, 'group', scatter_dimension=0, tiled=True)]
    dot_general x5 -> x0, matrix products: 74 us -> none  [the longest x2 54.2 us: body(): jnp.einsum('tij,tjf->tif', tiles, sources, precision=lax.Precision.HIGHEST)]
    unnamed x1 -> x0, blocking collectives: 48.7 us -> none
    ppermute x0 -> x32, starting transfers between devices: none -> 43.9 us  [send(): return lax.ppermute(value, AXES, pairs)]
    dot_general x4 -> x0, local copies, waits for them, and re-layouts: 38 us -> none  [the longest x2 25.4 us: body(): jnp.einsum('tij,tjf->tif', tiles, sources, precision=lax.Precision.HIGHEST)]
    pallas_call x0 -> x5, Pallas kernels: none -> 34.5 us  [the longest x4 20.8 us: products(): pl.pallas_call(functools.partial(product_kernel, first, n, rows), out_sha...]
  transfers between devices with their start and end apart: 4 -> 32, of which waited for: 4 -> 23; matrix products, arithmetic and copies ran while one was open for 2% -> 2% of each run, Pallas kernels for 0% -> 9%
where the time goes in v1:
time: 235 us; the launch traced here: 231 us
  waiting for transfers between devices  141 us (60%)
  starting transfers between devices  43.9 us (19%)
  Pallas kernels  34.5 us (15%)
  local copies, waits for them, and re-layouts  6.13 us (3%)
  other arithmetic  2.35 us (1%)
    ppermute x32, waiting for transfers between devices, send(): return lax.ppermute(value, AXES, pairs)  141 us
    ppermute x32, starting transfers between devices, send(): return lax.ppermute(value, AXES, pairs)  43.9 us
    pallas_call x4, Pallas kernels, products(): pl.pallas_call(functools.partial(product_kernel, first, n, rows), out_sha...  20.8 us
    pallas_call x1, Pallas kernels, prepare(): pl.pallas_call(prepare_kernel, out_shape=(jax.ShapeDtypeStruct((SLOTS,),...  13.7 us
  transfers between devices with their start and end apart: 32, of which 23 were waited for; matrix products, arithmetic and copies ran while one was open for 2% of the time, Pallas kernels for 9%

profile of v1, /device:TPU:24, one launch (start us, length us, event | category | flops | bytes accessed | tf_op | source)
XLA Modules:
  0.0 231.2 jit_solution(12089584854072418628)
XLA Ops:
  9.3 3.8 %collective-permute-done.1 = f32[384,256]{1,0:T(8,128)S(1)} collective-permute-done((f32[384,256]{1,0:T(8,128)}, f32[384,256]{1,0:T(8,128)S(1)}, u32[]{:S(2)}, u32[]{:S(2)}) %collective-permute-start.1) | collective-permute-done | bytes 393248 | tf_op jit(solution)/shard_map/ppermute | solution.py:54
  16.5 18.4 %collective-permute-done.3.refs_1_ = f32[1536,256]{1,0:T(8,128)S(1)} collective-permute-done((f32[1536,256]{1,0:T(8,128)S(1)}, f32[1536,256]{1,0:T(8,128)S(1)}, u32[]{:S(2)}, u32[]{:S(2)}) %collective-permute-start.3) | collective-permute-done | bytes 1572896 | tf_op jit(solution)/shard_map/ppermute | solution.py:54
  42.9 13.7 %prepare.1 = (s32[112]{0:T(128)S(1)}, s32[112]{0:T(128)S(1)}, s32[8]{0:T(128)S(1)}, s32[112]{0:T(128)}, bf16[112,128,256]{2,1,0:T(8,128)(2,1)S(1)}, /*index=5*/f32[16,8,128]{2,1,0:T(8,128)S(1)}) custom-call(s32[4]{0:T(128)S(1)} %pad_add_fusion.place, s32[96]{0:T(128)S(1)} %copy-done.3, s32[96]{0:T(128)S(1)} %copy-done.4, s32[32]{0:T(128)S(1)} %reshape.43.mirror, ...), custom_call_target="tpu_custom_call" | custom-call | flops 100000000 | bytes 13000000 | tf_op jit(solution)/shard_map/prepare/pallas_call | solution.py:166
  56.6 7.2 %late.2 = (f32[6,392,256]{2,1,0:T(8,128)S(1)}, f32[6,392,256]{2,1,0:T(8,128)S(1)}) custom-call(s32[112]{0:T(128)S(1)} %get-tuple-element.18.source, s32[112]{0:T(128)S(1)} %get-tuple-element.19.dest, s32[8]{0:T(128)S(1)} %get-tuple-element.20.bounds, f32[16,8,128]{2,1,0:T(8,128)S(1)} %get-tuple-element.21.degree, ...), custom_call_target="tpu_custom_call" | custom-call | flops 3000000000 | bytes 15000000 | tf_op jit(solution)/shard_map/late/pallas_call | solution.py:228
  64.7 4.1 %early.2 = (f32[2,392,256]{2,1,0:T(8,128)S(1)}, f32[2,392,256]{2,1,0:T(8,128)S(1)}) custom-call(s32[112]{0:T(128)S(1)} %get-tuple-element.18.source, s32[112]{0:T(128)S(1)} %get-tuple-element.19.dest, s32[8]{0:T(128)S(1)} %get-tuple-element.20.bounds, f32[16,8,128]{2,1,0:T(8,128)S(1)} %get-tuple-element.21.degree, ...), custom_call_target="tpu_custom_call" | custom-call | flops 1000000000 | bytes 15000000 | tf_op jit(solution)/shard_map/early/pallas_call | solution.py:228
  72.7 6.4 %collective-permute-start.13 = (f32[392,256]{1,0:T(8,128)S(1)}, f32[392,256]{1,0:T(8,128)S(1)}, u32[]{:S(2)}, u32[]{:S(2)}) collective-permute-start(f32[392,256]{1,0:T(8,128)S(1)} %get-tuple-element.39), channel_id=1, source_target_pairs={{0,224},{1,225},{2,226},{3,227},{4,228},{5,229},{6,230},{7,231},{8... | collective-permute-start | bytes 1204232 | tf_op jit(solution)/shard_map/ppermute | solution.py:54
  79.1 7.9 %collective-permute-done.8 = f32[392,256]{1,0:T(8,128)S(1)} collective-permute-done((f32[392,256]{1,0:T(8,128)S(1)}, f32[392,256]{1,0:T(8,128)S(1)}, u32[]{:S(2)}, u32[]{:S(2)}) %collective-permute-start.8) | collective-permute-done | bytes 401440 | tf_op jit(solution)/shard_map/ppermute | solution.py:54
  87.8 8.9 %collective-permute-done.10 = f32[392,256]{1,0:T(8,128)S(1)} collective-permute-done((f32[392,256]{1,0:T(8,128)S(1)}, f32[392,256]{1,0:T(8,128)S(1)}, u32[]{:S(2)}, u32[]{:S(2)}) %collective-permute-start.10) | collective-permute-done | bytes 401440 | tf_op jit(solution)/shard_map/ppermute | solution.py:54
  99.1 9.0 %collective-permute-done.14 = f32[392,256]{1,0:T(8,128)S(1)} collective-permute-done((f32[392,256]{1,0:T(8,128)S(1)}, f32[392,256]{1,0:T(8,128)S(1)}, u32[]{:S(2)}, u32[]{:S(2)}) %collective-permute-start.14) | collective-permute-done | bytes 401440 | tf_op jit(solution)/shard_map/ppermute | solution.py:54
  108.8 3.3 %collective-permute-start.15 = (f32[392,256]{1,0:T(8,128)S(1)}, f32[392,256]{1,0:T(8,128)S(1)}, u32[]{:S(2)}, u32[]{:S(2)}) collective-permute-start(f32[392,256]{1,0:T(8,128)S(1)} %get-tuple-element.31), channel_id=1, source_target_pairs={{0,224},{1,225},{2,226},{3,227},{4,228},{5,229},{6,230},{7,231},{8... | collective-permute-start | bytes 1204232 | tf_op jit(solution)/shard_map/ppermute | solution.py:54
  112.6 8.0 %collective-permute-done.12 = f32[392,256]{1,0:T(8,128)S(1)} collective-permute-done((f32[392,256]{1,0:T(8,128)S(1)}, f32[392,256]{1,0:T(8,128)S(1)}, u32[]{:S(2)}, u32[]{:S(2)}) %collective-permute-start.12) | collective-permute-done | bytes 401440 | tf_op jit(solution)/shard_map/ppermute | solution.py:54
  122.6 3.7 %collective-permute-start.17 = (f32[384,256]{1,0:T(8,128)S(1)}, f32[384,256]{1,0:T(8,128)S(1)}, u32[]{:S(2)}, u32[]{:S(2)}) collective-permute-start(f32[384,256]{1,0:T(8,128)S(1)} %broadcast_multiply_fusion.1), channel_id=1, source_target_pairs={{0,12},{1,13},{2,14},{3,15},{4,0},{5,1},{6,2},{7,3},{8,4},{9,5},{1... | collective-permute-start | bytes 1179656 | tf_op jit(solution)/shard_map/ppermute | solution.py:54
  126.3 4.6 %collective-permute-done.18 = f32[384,256]{1,0:T(8,128)S(1)} collective-permute-done((f32[384,256]{1,0:T(8,128)S(1)}, f32[384,256]{1,0:T(8,128)S(1)}, u32[]{:S(2)}, u32[]{:S(2)}) %collective-permute-start.18) | collective-permute-done | bytes 393248 | tf_op jit(solution)/shard_map/ppermute | solution.py:54
  130.9 4.8 %collective-permute-done.17 = f32[384,256]{1,0:T(8,128)S(1)} collective-permute-done((f32[384,256]{1,0:T(8,128)S(1)}, f32[384,256]{1,0:T(8,128)S(1)}, u32[]{:S(2)}, u32[]{:S(2)}) %collective-permute-start.17) | collective-permute-done | bytes 393248 | tf_op jit(solution)/shard_map/ppermute | solution.py:54
  137.9 18.4 %collective-permute-done.19.refs_1_ = f32[1536,256]{1,0:T(8,128)S(1)} collective-permute-done((f32[1536,256]{1,0:T(8,128)S(1)}, f32[1536,256]{1,0:T(8,128)S(1)}, u32[]{:S(2)}, u32[]{:S(2)}) %collective-permute-start.19) | collective-permute-done | bytes 1572896 | tf_op jit(solution)/shard_map/ppermute | solution.py:54
  158.6 9.8 %collective-permute-done.21.refs_3_ = f32[768,256]{1,0:T(8,128)S(1)} collective-permute-done((f32[768,256]{1,0:T(8,128)S(1)}, f32[768,256]{1,0:T(8,128)S(1)}, u32[]{:S(2)}, u32[]{:S(2)}) %collective-permute-start.21) | collective-permute-done | bytes 786464 | tf_op jit(solution)/shard_map/ppermute | solution.py:54
  171.5 6.3 %late.3 = (f32[6,384,256]{2,1,0:T(8,128)S(1)}, f32[6,384,256]{2,1,0:T(8,128)S(1)}) custom-call(s32[112]{0:T(128)S(1)} %get-tuple-element.18.source, s32[112]{0:T(128)S(1)} %get-tuple-element.19.dest, s32[8]{0:T(128)S(1)} %get-tuple-element.20.bounds, f32[16,8,128]{2,1,0:T(8,128)S(1)} %get-tuple-element.21.degree, ...), custom_call_target="tpu_custom_call" | custom-call | flops 3000000000 | bytes 15000000 | tf_op jit(solution)/shard_map/late/pallas_call | solution.py:228
  177.9 3.2 %early.3 = (f32[2,384,256]{2,1,0:T(8,128)S(1)}, f32[2,384,256]{2,1,0:T(8,128)S(1)}) custom-call(s32[112]{0:T(128)S(1)} %get-tuple-element.18.source, s32[112]{0:T(128)S(1)} %get-tuple-element.19.dest, s32[8]{0:T(128)S(1)} %get-tuple-element.20.bounds, f32[16,8,128]{2,1,0:T(8,128)S(1)} %get-tuple-element.21.degree, ...), custom_call_target="tpu_custom_call" | custom-call | flops 1000000000 | bytes 15000000 | tf_op jit(solution)/shard_map/early/pallas_call | solution.py:228
  184.0 4.8 %collective-permute-start.29 = (f32[384,256]{1,0:T(8,128)S(1)}, f32[384,256]{1,0:T(8,128)S(1)}, u32[]{:S(2)}, u32[]{:S(2)}) collective-permute-start(f32[384,256]{1,0:T(8,128)S(1)} %get-tuple-element.41), channel_id=1, source_target_pairs={{0,224},{1,225},{2,226},{3,227},{4,228},{5,229},{6,230},{7,231},{8... | collective-permute-start | bytes 1179656 | tf_op jit(solution)/shard_map/ppermute | solution.py:54
  188.8 7.7 %collective-permute-done.24 = f32[384,256]{1,0:T(8,128)S(1)} collective-permute-done((f32[384,256]{1,0:T(8,128)S(1)}, f32[384,256]{1,0:T(8,128)S(1)}, u32[]{:S(2)}, u32[]{:S(2)}) %collective-permute-start.24) | collective-permute-done | bytes 393248 | tf_op jit(solution)/shard_map/ppermute | solution.py:54
  197.4 8.5 %collective-permute-done.26 = f32[384,256]{1,0:T(8,128)S(1)} collective-permute-done((f32[384,256]{1,0:T(8,128)S(1)}, f32[384,256]{1,0:T(8,128)S(1)}, u32[]{:S(2)}, u32[]{:S(2)}) %collective-permute-start.26) | collective-permute-done | bytes 393248 | tf_op jit(solution)/shard_map/ppermute | solution.py:54
  208.1 9.0 %collective-permute-done.30 = f32[384,256]{1,0:T(8,128)S(1)} collective-permute-done((f32[384,256]{1,0:T(8,128)S(1)}, f32[384,256]{1,0:T(8,128)S(1)}, u32[]{:S(2)}, u32[]{:S(2)}) %collective-permute-start.30) | collective-permute-done | bytes 393248 | tf_op jit(solution)/shard_map/ppermute | solution.py:54
  218.0 3.2 %collective-permute-start.31 = (f32[384,256]{1,0:T(8,128)S(1)}, f32[384,256]{1,0:T(8,128)S(1)}, u32[]{:S(2)}, u32[]{:S(2)}) collective-permute-start(f32[384,256]{1,0:T(8,128)S(1)} %get-tuple-element.35), channel_id=1, source_target_pairs={{0,224},{1,225},{2,226},{3,227},{4,228},{5,229},{6,230},{7,231},{8... | collective-permute-start | bytes 1179656 | tf_op jit(solution)/shard_map/ppermute | solution.py:54
  221.7 7.9 %collective-permute-done.28 = f32[384,256]{1,0:T(8,128)S(1)} collective-permute-done((f32[384,256]{1,0:T(8,128)S(1)}, f32[384,256]{1,0:T(8,128)S(1)}, u32[]{:S(2)}, u32[]{:S(2)}) %collective-permute-start.28) | collective-permute-done | bytes 393248 | tf_op jit(solution)/shard_map/ppermute | solution.py:54
  (93 shorter events, 47.6 us)
Async XLA Ops:
  1.5 11.6 %collective-permute-start.1 = (f32[384,256]{1,0:T(8,128)}, f32[384,256]{1,0:T(8,128)S(1)}, u32[]{:S(2)}, u32[]{:S(2)}) collective-permute-start(f32[384,256]{1,0:T(8,128)} %param.8), channel_id=1, source_target_pairs={{0,12},{1,13},{2,14},{3,15},{4,0},{5,1},{6,2},{7,3},{8,4},{9,5},{1... | collective-permute-start | bytes 1179656 | tf_op jit(solution)/shard_map/ppermute | solution.py:54
  3.2 11.2 %collective-permute-start.2 = (f32[384,256]{1,0:T(8,128)}, f32[384,256]{1,0:T(8,128)S(1)}, u32[]{:S(2)}, u32[]{:S(2)}) collective-permute-start(f32[384,256]{1,0:T(8,128)} %param.8), channel_id=1, source_target_pairs={{0,8},{1,9},{2,10},{3,11},{4,12},{5,13},{6,14},{7,15},{8,0},{9,1},... | collective-permute-start | bytes 1179656 | tf_op jit(solution)/shard_map/ppermute | solution.py:54
  14.4 20.5 %collective-permute-start.3 = (f32[1536,256]{1,0:T(8,128)S(1)}, f32[1536,256]{1,0:T(8,128)S(1)}, u32[]{:S(2)}, u32[]{:S(2)}) collective-permute-start(f32[1536,256]{1,0:T(8,128)S(1)} %constant_dynamic-update-slice_fusion.refs_0_), channel_id=1, source_target_pairs={{0,1},{1,2},{2,3},{3,0},{4,5},{5,6},{6,7},{7,4},{8,9},{9,10},{10,1... | collective-permute-start | bytes 4718600 | tf_op jit(solution)/shard_map/ppermute | solution.py:54
  15.6 22.6 %collective-permute-start.4 = (f32[1536,256]{1,0:T(8,128)S(1)}, f32[1536,256]{1,0:T(8,128)S(1)}, u32[]{:S(2)}, u32[]{:S(2)}) collective-permute-start(f32[1536,256]{1,0:T(8,128)S(1)} %constant_dynamic-update-slice_fusion.refs_0_), channel_id=1, source_target_pairs={{0,3},{1,0},{2,1},{3,2},{4,7},{5,4},{6,5},{7,6},{8,11},{9,8},{10,9... | collective-permute-start | bytes 4718600 | tf_op jit(solution)/shard_map/ppermute | solution.py:54
  35.9 20.7 %collective-permute-start.5 = (f32[768,256]{1,0:T(8,128)}, f32[768,256]{1,0:T(8,128)}, u32[]{:S(2)}, u32[]{:S(2)}) collective-permute-start(f32[768,256]{1,0:T(8,128)} %slice.168), channel_id=1, source_target_pairs={{0,1},{1,2},{2,3},{3,0},{4,5},{5,6},{6,7},{7,4},{8,9},{9,10},{10,1... | collective-permute-start | bytes 2359304 | tf_op jit(solution)/shard_map/ppermute | solution.py:54
  39.1 17.4 %collective-permute-start.6 = (f32[768,256]{1,0:T(8,128)}, f32[768,256]{1,0:T(8,128)}, u32[]{:S(2)}, u32[]{:S(2)}) collective-permute-start(f32[768,256]{1,0:T(8,128)} %slice.169), channel_id=1, source_target_pairs={{0,3},{1,0},{2,1},{3,2},{4,7},{5,4},{6,5},{7,6},{8,11},{9,8},{10,9... | collective-permute-start | bytes 2359304 | tf_op jit(solution)/shard_map/ppermute | solution.py:54
  63.8 23.2 %collective-permute-start.9 = (f32[6,392,256]{2,1,0:T(8,128)S(1)}, f32[6,392,256]{2,1,0:T(8,128)S(1)}, u32[]{:S(2)}, u32[]{:S(2)}) collective-permute-start(f32[6,392,256]{2,1,0:T(8,128)S(1)} %get-tuple-element.26), channel_id=1, source_target_pairs={{0,16},{1,17},{2,18},{3,19},{4,20},{5,21},{6,22},{7,23},{8,24},{9,... | collective-permute-start | bytes 7225352 | tf_op jit(solution)/shard_map/ppermute | solution.py:54
  71.2 15.7 %collective-permute-start.8 = (f32[392,256]{1,0:T(8,128)S(1)}, f32[392,256]{1,0:T(8,128)S(1)}, u32[]{:S(2)}, u32[]{:S(2)}) collective-permute-start(f32[392,256]{1,0:T(8,128)S(1)} %get-tuple-element.40), channel_id=1, source_target_pairs={{0,32},{1,33},{2,34},{3,35},{4,36},{5,37},{6,38},{7,39},{8,40},{9,... | collective-permute-start | bytes 1204232 | tf_op jit(solution)/shard_map/ppermute | solution.py:54
  72.7 15.2 %collective-permute-start.13 = (f32[392,256]{1,0:T(8,128)S(1)}, f32[392,256]{1,0:T(8,128)S(1)}, u32[]{:S(2)}, u32[]{:S(2)}) collective-permute-start(f32[392,256]{1,0:T(8,128)S(1)} %get-tuple-element.39), channel_id=1, source_target_pairs={{0,224},{1,225},{2,226},{3,227},{4,228},{5,229},{6,230},{7,231},{8... | collective-permute-start | bytes 1204232 | tf_op jit(solution)/shard_map/ppermute | solution.py:54
  87.0 9.7 %collective-permute-start.10 = (f32[392,256]{1,0:T(8,128)S(1)}, f32[392,256]{1,0:T(8,128)S(1)}, u32[]{:S(2)}, u32[]{:S(2)}) collective-permute-start(f32[392,256]{1,0:T(8,128)S(1)} %fusion.15), channel_id=1, source_target_pairs={{0,32},{1,33},{2,34},{3,35},{4,36},{5,37},{6,38},{7,39},{8,40},{9,... | collective-permute-start | bytes 1204232 | tf_op jit(solution)/shard_map/ppermute | solution.py:54
  97.0 11.1 %collective-permute-start.14 = (f32[392,256]{1,0:T(8,128)S(1)}, f32[392,256]{1,0:T(8,128)S(1)}, u32[]{:S(2)}, u32[]{:S(2)}) collective-permute-start(f32[392,256]{1,0:T(8,128)S(1)} %get-tuple-element.33), channel_id=1, source_target_pairs={{0,224},{1,225},{2,226},{3,227},{4,228},{5,229},{6,230},{7,231},{8... | collective-permute-start | bytes 1204232 | tf_op jit(solution)/shard_map/ppermute | solution.py:54
  108.7 11.9 %collective-permute-start.12 = (f32[392,256]{1,0:T(8,128)S(1)}, f32[392,256]{1,0:T(8,128)S(1)}, u32[]{:S(2)}, u32[]{:S(2)}) collective-permute-start(f32[392,256]{1,0:T(8,128)S(1)} %get-tuple-element.32), channel_id=1, source_target_pairs={{0,32},{1,33},{2,34},{3,35},{4,36},{5,37},{6,38},{7,39},{8,40},{9,... | collective-permute-start | bytes 1204232 | tf_op jit(solution)/shard_map/ppermute | solution.py:54
  108.8 11.8 %collective-permute-start.15 = (f32[392,256]{1,0:T(8,128)S(1)}, f32[392,256]{1,0:T(8,128)S(1)}, u32[]{:S(2)}, u32[]{:S(2)}) collective-permute-start(f32[392,256]{1,0:T(8,128)S(1)} %get-tuple-element.31), channel_id=1, source_target_pairs={{0,224},{1,225},{2,226},{3,227},{4,228},{5,229},{6,230},{7,231},{8... | collective-permute-start | bytes 1204232 | tf_op jit(solution)/shard_map/ppermute | solution.py:54
  122.6 13.1 %collective-permute-start.17 = (f32[384,256]{1,0:T(8,128)S(1)}, f32[384,256]{1,0:T(8,128)S(1)}, u32[]{:S(2)}, u32[]{:S(2)}) collective-permute-start(f32[384,256]{1,0:T(8,128)S(1)} %broadcast_multiply_fusion.1), channel_id=1, source_target_pairs={{0,12},{1,13},{2,14},{3,15},{4,0},{5,1},{6,2},{7,3},{8,4},{9,5},{1... | collective-permute-start | bytes 1179656 | tf_op jit(solution)/shard_map/ppermute | solution.py:54
  135.8 20.5 %collective-permute-start.19 = (f32[1536,256]{1,0:T(8,128)S(1)}, f32[1536,256]{1,0:T(8,128)S(1)}, u32[]{:S(2)}, u32[]{:S(2)}) collective-permute-start(f32[1536,256]{1,0:T(8,128)S(1)} %pad_maximum_fusion.refs_0_), channel_id=1, source_target_pairs={{0,1},{1,2},{2,3},{3,0},{4,5},{5,6},{6,7},{7,4},{8,9},{9,10},{10,1... | collective-permute-start | bytes 4718600 | tf_op jit(solution)/shard_map/ppermute | solution.py:54
  136.4 21.8 %collective-permute-start.20 = (f32[1536,256]{1,0:T(8,128)S(1)}, f32[1536,256]{1,0:T(8,128)S(1)}, u32[]{:S(2)}, u32[]{:S(2)}) collective-permute-start(f32[1536,256]{1,0:T(8,128)S(1)} %pad_maximum_fusion.refs_0_), channel_id=1, source_target_pairs={{0,3},{1,0},{2,1},{3,2},{4,7},{5,4},{6,5},{7,6},{8,11},{9,8},{10,9... | collective-permute-start | bytes 4718600 | tf_op jit(solution)/shard_map/ppermute | solution.py:54
  156.3 12.1 %collective-permute-start.21 = (f32[768,256]{1,0:T(8,128)S(1)}, f32[768,256]{1,0:T(8,128)S(1)}, u32[]{:S(2)}, u32[]{:S(2)}) collective-permute-start(f32[768,256]{1,0:T(8,128)S(1)} %slice.180), channel_id=1, source_target_pairs={{0,1},{1,2},{2,3},{3,0},{4,5},{5,6},{6,7},{7,4},{8,9},{9,10},{10,1... | collective-permute-start | bytes 2359304 | tf_op jit(solution)/shard_map/ppermute | solution.py:54
  158.2 13.3 %collective-permute-start.22 = (f32[768,256]{1,0:T(8,128)S(1)}, f32[768,256]{1,0:T(8,128)S(1)}, u32[]{:S(2)}, u32[]{:S(2)}) collective-permute-start(f32[768,256]{1,0:T(8,128)S(1)} %slice.181), channel_id=1, source_target_pairs={{0,3},{1,0},{2,1},{3,2},{4,7},{5,4},{6,5},{7,6},{8,11},{9,8},{10,9... | collective-permute-start | bytes 2359304 | tf_op jit(solution)/shard_map/ppermute | solution.py:54
  177.8 18.7 %collective-permute-start.25 = (f32[6,384,256]{2,1,0:T(8,128)S(1)}, f32[6,384,256]{2,1,0:T(8,128)S(1)}, u32[]{:S(2)}, u32[]{:S(2)}) collective-permute-start(f32[6,384,256]{2,1,0:T(8,128)S(1)} %get-tuple-element.30), channel_id=1, source_target_pairs={{0,16},{1,17},{2,18},{3,19},{4,20},{5,21},{6,22},{7,23},{8,24},{9,... | collective-permute-start | bytes 7077896 | tf_op jit(solution)/shard_map/ppermute | solution.py:54
  183.6 12.8 %collective-permute-start.24 = (f32[384,256]{1,0:T(8,128)S(1)}, f32[384,256]{1,0:T(8,128)S(1)}, u32[]{:S(2)}, u32[]{:S(2)}) collective-permute-start(f32[384,256]{1,0:T(8,128)S(1)} %get-tuple-element.42), channel_id=1, source_target_pairs={{0,32},{1,33},{2,34},{3,35},{4,36},{5,37},{6,38},{7,39},{8,40},{9,... | collective-permute-start | bytes 1179656 | tf_op jit(solution)/shard_map/ppermute | solution.py:54
  184.0 13.4 %collective-permute-start.29 = (f32[384,256]{1,0:T(8,128)S(1)}, f32[384,256]{1,0:T(8,128)S(1)}, u32[]{:S(2)}, u32[]{:S(2)}) collective-permute-start(f32[384,256]{1,0:T(8,128)S(1)} %get-tuple-element.41), channel_id=1, source_target_pairs={{0,224},{1,225},{2,226},{3,227},{4,228},{5,229},{6,230},{7,231},{8... | collective-permute-start | bytes 1179656 | tf_op jit(solution)/shard_map/ppermute | solution.py:54
  206.0 11.1 %collective-permute-start.30 = (f32[384,256]{1,0:T(8,128)S(1)}, f32[384,256]{1,0:T(8,128)S(1)}, u32[]{:S(2)}, u32[]{:S(2)}) collective-permute-start(f32[384,256]{1,0:T(8,128)S(1)} %get-tuple-element.37), channel_id=1, source_target_pairs={{0,224},{1,225},{2,226},{3,227},{4,228},{5,229},{6,230},{7,231},{8... | collective-permute-start | bytes 1179656 | tf_op jit(solution)/shard_map/ppermute | solution.py:54
  217.9 11.7 %collective-permute-start.28 = (f32[384,256]{1,0:T(8,128)S(1)}, f32[384,256]{1,0:T(8,128)S(1)}, u32[]{:S(2)}, u32[]{:S(2)}) collective-permute-start(f32[384,256]{1,0:T(8,128)S(1)} %get-tuple-element.36), channel_id=1, source_target_pairs={{0,32},{1,33},{2,34},{3,35},{4,36},{5,37},{6,38},{7,39},{8,40},{9,... | collective-permute-start | bytes 1179656 | tf_op jit(solution)/shard_map/ppermute | solution.py:54
  218.0 11.6 %collective-permute-start.31 = (f32[384,256]{1,0:T(8,128)S(1)}, f32[384,256]{1,0:T(8,128)S(1)}, u32[]{:S(2)}, u32[]{:S(2)}) collective-permute-start(f32[384,256]{1,0:T(8,128)S(1)} %get-tuple-element.35), channel_id=1, source_target_pairs={{0,224},{1,225},{2,226},{3,227},{4,228},{5,229},{6,230},{7,231},{8... | collective-permute-start | bytes 1179656 | tf_op jit(solution)/shard_map/ppermute | solution.py:54
  (17 other events, 245.2 us)
